TPU v7x, 256 devices: a whole 4x4x8 slice. The times are simulated.
256 devices in a mesh: row: 8 (over x, z_hi), col: 32 (over z_lo, y, core).
Axes of the slice: x: 4, y: 4, z: 8 (z_hi: 2, z_lo: 4; z = z_hi * 4 + z_lo), core: 2. Of those that a mesh axis runs over, the one named last changes fastest.
Arguments:
- inputs: bfloat16 [512, 8192], P('col', 'row'), may hold values from -6 to 6
- out_grad: bfloat16 [512, 8192], P('col', 'row'), may hold values from -1.5 to 1.5
- gate_weight: bfloat16 [8192, 28672], P('row', 'col'), may hold values from -0.0625 to 0.0625
- up_weight: bfloat16 [8192, 28672], P('row', 'col'), may hold values from -0.0625 to 0.0625
- down_weight: bfloat16 [28672, 8192], P('col', 'row'), may hold values from -0.03125 to 0.03125
Outputs:
- input_grad: bfloat16 [512, 8192], P('col', 'row')
- gate_weight_grad: bfloat16 [8192, 28672], P('row', 'col')
- up_weight_grad: bfloat16 [8192, 28672], P('row', 'col')
- down_weight_grad: bfloat16 [28672, 8192], P('col', 'row')
All inputs are finite; a program needn't handle non-finite values.
Results may differ from a plain program's by a relative error of at most 0.005.
Values may be sent and summed in bfloat16 or wider, within the bound.
A program may use at most 64 MiB of HBM per device.

v0:
```python
import jax
import jax.numpy as jnp
from jax import lax
from jax.sharding import PartitionSpec as P


def local_grads(gate, up, hidden_grad):
    sigm = jax.nn.sigmoid(gate)
    act = gate * sigm
    hidden = (act * up).astype(jnp.bfloat16)
    up_grad = (hidden_grad * act).astype(jnp.bfloat16)
    gate_grad = (hidden_grad * up * sigm * (1.0 + gate * (1.0 - sigm))).astype(jnp.bfloat16)
    return (hidden, gate_grad, up_grad)


def body(inputs, out_grad, gate_weight, up_weight, down_weight):
    inputs_all, grad_all = (
        lax.all_gather(inputs, "col", axis=0, tiled=True),
        lax.all_gather(out_grad, "col", axis=0, tiled=True),
    )
    gate_part = jnp.dot(inputs_all, gate_weight, preferred_element_type=jnp.float32)
    up_part = jnp.dot(inputs_all, up_weight, preferred_element_type=jnp.float32)
    hidden_part = lax.dot_general(
        grad_all, down_weight, (((1,), (1,)), ((), ())), preferred_element_type=jnp.float32
    )
    gate, up, hidden_grad = (
        lax.psum_scatter(gate_part, "row", scatter_dimension=0, tiled=True),
        lax.psum_scatter(up_part, "row", scatter_dimension=0, tiled=True),
        lax.psum_scatter(hidden_part, "row", scatter_dimension=0, tiled=True),
    )
    hidden, gate_grad, up_grad = local_grads(gate, up, hidden_grad)
    hidden, gate_grad, up_grad = (
        lax.all_gather(hidden, "row", axis=0, tiled=True),
        lax.all_gather(gate_grad, "row", axis=0, tiled=True),
        lax.all_gather(up_grad, "row", axis=0, tiled=True),
    )
    contract_rows = (((0,), (0,)), ((), ()))
    down_weight_grad = lax.dot_general(
        hidden, grad_all, contract_rows, preferred_element_type=jnp.float32
    ).astype(jnp.bfloat16)
    gate_weight_grad = lax.dot_general(
        inputs_all, gate_grad, contract_rows, preferred_element_type=jnp.float32
    ).astype(jnp.bfloat16)
    up_weight_grad = lax.dot_general(
        inputs_all, up_grad, contract_rows, preferred_element_type=jnp.float32
    ).astype(jnp.bfloat16)
    contract_units = (((1,), (1,)), ((), ()))
    first = lax.dot_general(
        gate_grad, gate_weight, contract_units, preferred_element_type=jnp.float32
    )
    second = lax.dot_general(up_grad, up_weight, contract_units, preferred_element_type=jnp.float32)
    input_grad = lax.psum_scatter(first + second, "col", scatter_dimension=0, tiled=True).astype(
        jnp.bfloat16
    )
    return (input_grad, gate_weight_grad, up_weight_grad, down_weight_grad)


def solution(mesh):
    return jax.shard_map(
        body,
        mesh=mesh,
        in_specs=(
            P("col", "row"),
            P("col", "row"),
            P("row", "col"),
            P("row", "col"),
            P("col", "row"),
        ),
        out_specs=(P("col", "row"), P("row", "col"), P("row", "col"), P("col", "row")),
        check_vma=False,
    )
```

profile of v0, /device:TPU:1, one launch (start us, length us, event | category | flops | bytes accessed | tf_op | source)
XLA Modules:
  0.0 683.8 jit_solution(5841717833502296948)
XLA Ops:
  8.0 0.7 all-gather.3.cloned.1.call-update
  8.7 64.3 %all-gather.5.cloned.1.call-done = bf16[512,1024]{1,0:T(8,128)(2,1)} async-done(((bf16[16,1024]{1,0:T(8,128)(2,1)}), bf16[512,1024]{1,0:T(8,128)(2,1)}) %all-gather.5.cloned.1.call-update) | async-done | bytes 1048592 | tf_op jit(solution)/shard_map/all_gather | solution.py:18
  73.0 4.3 fusion.2
  77.4 1.1 copy-done.3
  78.6 2.5 fusion.3
  81.1 51.6 %all-gather.3.cloned.1.call-done = bf16[512,1024]{1,0:T(8,128)(2,1)} async-done(((bf16[16,1024]{1,0:T(8,128)(2,1)}), bf16[512,1024]{1,0:T(8,128)(2,1)}) %all-gather.3.cloned.1.call-update) | async-done | bytes 1048592 | tf_op jit(solution)/shard_map/all_gather | solution.py:19
  132.7 4.3 fusion.1
  137.1 90.0 %reduce-scatter.7.cloned.1.call-done = f32[64,896]{1,0:T(8,128)} async-done(((f32[512,896]{1,0:T(8,128)}), f32[64,896]{1,0:T(8,128)}) %reduce-scatter.7.cloned.1.call-update) | async-done | bytes 229392 | tf_op jit(solution)/shard_map/reduce_scatter | solution.py:28
  227.1 93.0 %reduce-scatter.9.cloned.1.call-done = f32[64,896]{1,0:T(8,128)} async-done(((f32[512,896]{1,0:T(8,128)}), f32[64,896]{1,0:T(8,128)}) %reduce-scatter.9.cloned.1.call-update) | async-done | bytes 229392 | tf_op jit(solution)/shard_map/reduce_scatter | solution.py:27
  320.1 93.0 %reduce-scatter.5.cloned.1.call-done = f32[64,896]{1,0:T(8,128)} async-done(((f32[512,896]{1,0:T(8,128)}), f32[64,896]{1,0:T(8,128)}) %reduce-scatter.5.cloned.1.call-update) | async-done | bytes 229392 | tf_op jit(solution)/shard_map/reduce_scatter | solution.py:29
  413.1 1.3 multiply_convert_fusion
  414.4 49.0 %all_gather.17 = bf16[512,896]{1,0:T(8,128)(2,1)S(1)} all-gather(bf16[64,896]{1,0:T(8,128)(2,1)S(1)} %get-tuple-element.9), channel_id=1, replica_groups=mesh['row'=8,'col'=32] {'row'}, dimensions={0}, use_global_device_ids=true | all-gather | bytes 1032192 | tf_op jit(solution)/shard_map/all_gather | solution.py:34
  463.3 1.3 fusion.4
  464.6 48.5 %all_gather.18 = bf16[512,896]{1,0:T(8,128)(2,1)S(1)} all-gather(bf16[64,896]{1,0:T(8,128)(2,1)S(1)} %get-tuple-element.10), channel_id=1, replica_groups=mesh['row'=8,'col'=32] {'row'}, dimensions={0}, use_global_device_ids=true | all-gather | bytes 1032192 | tf_op jit(solution)/shard_map/all_gather | solution.py:35
  513.1 0.9 copy-done.1
  514.1 2.6 convolution_add_fusion
  516.7 3.9 convert_bitcast_fusion
  520.6 3.8 copy.10
  524.4 3.6 convert_bitcast_fusion.1
  528.0 3.9 copy.9
  531.9 52.9 %all_gather.19 = bf16[512,896]{1,0:T(8,128)(2,1)S(1)} all-gather(bf16[64,896]{1,0:T(8,128)(2,1)S(1)} %get-tuple-element.8), channel_id=1, replica_groups=mesh['row'=8,'col'=32] {'row'}, dimensions={0}, use_global_device_ids=true | all-gather | bytes 1032192 | tf_op jit(solution)/shard_map/all_gather | solution.py:33
  584.7 2.4 convolution_convert_fusion
  587.1 88.3 %reduce-scatter.11.cloned.1.call-done = f32[16,1024]{1,0:T(8,128)} async-done(((f32[512,1024]{1,0:T(8,128)}), f32[16,1024]{1,0:T(8,128)}) %reduce-scatter.11.cloned.1.call-update) | async-done | bytes 65552 | tf_op jit(solution)/shard_map/reduce_scatter | solution.py:52
  675.5 1.5 convert_element_type.29
  (19 shorter events, 1.0 us)
Async XLA Ops:
  7.2 70.3 %copy-start = (bf16[1024,896]{1,0:T(8,128)(2,1)S(1)}, bf16[1024,896]{1,0:T(8,128)(2,1)}, u32[]{:S(2)}) copy-start(bf16[1024,896]{1,0:T(8,128)(2,1)} %param.7) | copy-start | bytes 5505028
  7.2 65.9 %all-gather.5.cloned.1.call-start = ((), (), s32[]{:S(2)}) async-start(), calls=%async_computation.6 | async-start | bytes 1081344 | tf_op jit(solution)/shard_map/all_gather | solution.py:18
  7.9 124.8 %all-gather.3.cloned.1.call-start = ((), (), s32[]{:S(2)}) async-start(), calls=%async_computation.4 | async-start | bytes 1081344 | tf_op jit(solution)/shard_map/all_gather | solution.py:19
  8.7 218.5 %reduce-scatter.7.cloned.1.call-start = ((), (), s32[]{:S(2)}) async-start(), calls=%async_computation.7 | async-start | bytes 2064384 | tf_op jit(solution)/shard_map/reduce_scatter | solution.py:28
  77.3 1.2 copy-start.3
  77.4 242.8 %reduce-scatter.9.cloned.1.call-start = ((), (), s32[]{:S(2)}) async-start(), calls=%async_computation.8 | async-start | bytes 2064384 | tf_op jit(solution)/shard_map/reduce_scatter | solution.py:27
  81.1 332.0 %reduce-scatter.5.cloned.1.call-start = ((), (), s32[]{:S(2)}) async-start(), calls=%async_computation.5 | async-start | bytes 2064384 | tf_op jit(solution)/shard_map/reduce_scatter | solution.py:29
  137.1 538.4 %reduce-scatter.11.cloned.1.call-start = ((), (), s32[]{:S(2)}) async-start(), calls=%async_computation.9 | async-start | bytes 2162688 | tf_op jit(solution)/shard_map/reduce_scatter | solution.py:52
  463.3 50.7 %copy-start.2 = (bf16[1024,896]{1,0:T(8,128)(2,1)S(1)}, bf16[1024,896]{1,0:T(8,128)(2,1)}, u32[]{:S(2)}) copy-start(bf16[1024,896]{1,0:T(8,128)(2,1)} %param.8) | copy-start | bytes 5505028
  513.1 0.9 copy-start.1
  528.0 56.8 %copy-start.4 = (bf16[512,1024]{1,0:T(8,128)(2,1)S(1)}, bf16[512,1024]{1,0:T(8,128)(2,1)}, u32[]{:S(2)}) copy-start(bf16[512,1024]{1,0:T(8,128)(2,1)} %all-gather.3.cloned.1.call-done) | copy-start | bytes 3145732
Sparse Core Ops, SparseCore 0:
  9.9 63.1 all-gather.4
  74.9 57.7 all-gather.2
  137.4 89.7 reduce-scatter.6
  231.6 88.4 reduce-scatter.8
  324.6 88.4 reduce-scatter.4
  516.8 158.5 reduce-scatter.10
where the time goes:
time: 688 us; the launch traced here: 684 us
  waiting for transfers between devices  482 us (70%)
  blocking collectives  150 us (22%)
  matrix products  24.9 us (4%)
  between operations  14.1 us (2%)
  local copies, waits for them, and re-layouts  9.76 us (1%)
    reduce_scatter x1, waiting for transfers between devices, body(): lax.psum_scatter(gate_part, 'row', scatter_dimension=0, tiled=True)  93 us
    reduce_scatter x1, waiting for transfers between devices, body(): lax.psum_scatter(hidden_part, 'row', scatter_dimension=0, tiled=True)  93 us
    reduce_scatter x1, waiting for transfers between devices, body(): lax.psum_scatter(up_part, 'row', scatter_dimension=0, tiled=True)  90 us
    reduce_scatter x1, waiting for transfers between devices, body(): lax.psum_scatter(first + second, 'col', scatter_dimension=0, tiled=True)  88.3 us
    all_gather x1, waiting for transfers between devices, body(): lax.all_gather(inputs, 'col', axis=0, tiled=True)  64.3 us
    all_gather x1, blocking collectives, body(): lax.all_gather(hidden, 'row', axis=0, tiled=True)  52.9 us
    all_gather x1, waiting for transfers between devices, body(): lax.all_gather(out_grad, 'col', axis=0, tiled=True)  51.6 us
    all_gather x1, blocking collectives, body(): lax.all_gather(gate_grad, 'row', axis=0, tiled=True)  49 us
  transfers between devices with their start and end apart: 6, of which 6 were waited for; matrix products, arithmetic and copies ran while one was open for 4% of the time, Pallas kernels for 0%

commit v1 on v0

v1 whole, which is shorter than its diff:
```python
import jax
import jax.numpy as jnp
from jax import lax
from jax.experimental import pallas as pl
from jax.experimental.pallas import tpu as pltpu
from jax.sharding import PartitionSpec as P

MESH = pl.DeviceIdType.MESH
BF16 = jnp.bfloat16
F32 = jnp.float32

CHUNKS = 8
CHUNK_OF = ((0, 0), (1, 0), (3, 0), (1, 1), (3, 1), (2, 0), (2, 1), (0, 1))
LAG_B, LAG_C, LAG_D, LAG_F, LAG_G, LAG_H = 1, 2, 5, 6, 7, 8

RELAY_LO, RELAY_HI, DIRECT_HI, DIRECT_LO, SUM_LO, SUM_HI, ZSUM = range(7)
OWN_UP_LO, OWN_UP_HI, OWN_DN_HI, OWN_DN_LO, FWD_LO, FWD_HI = range(7, 13)
PER_CHUNK = 13
NT = (((1,), (1,)), ((), ()))


def comm_kernel(
    x_hbm, dy_hbm, wg_hbm, wu_hbm, wd_hbm,
    ig_ref, xo_hbm, do_hbm, h_hbm, gg_hbm, ug_hbm,
    xd, wg, wu, wd, part, s_far, s_near, s_sum, s_z, r_relay, r_near, r_sum, r_z, grads,
    ig_part, ig_sib, ig_ysend, ig_yrecv, ig_msend, ig_mrecv, ig_zsend, ig_zrecv,
    load_sem, send, recv, p1_send, p1_recv, sib_send, sib_recv, y_send, y_recv,
    ig_sib_send, ig_sib_recv, ig_y_send, ig_y_recv, ig_z_send, ig_z_recv, out_sem,
):
    ff = wg.shape[1]
    width = 3 * ff
    cut = (width // 256) * 128
    lo, hi = pl.ds(0, cut), pl.ds(cut, width - cut)

    row, col = lax.axis_index("row"), lax.axis_index("col")
    x, zh = row // 2, row % 2
    zl, y, k = col // 8, (col // 2) % 4, col % 2
    zlo = zl % 2

    def dev(x=x, zh=zh, zl=zl, y=y, k=k):
        return (x * 2 + zh, zl * 8 + y * 2 + k)

    xp, xm, xf = (x + 1) % 4, (x + 3) % 4, (x + 2) % 4
    up, down = dev(x=xp), dev(x=xm)
    partner = dev(zh=1 - zh)
    yp, ym, yf = dev(y=(y + 1) % 4), dev(y=(y + 3) % 4), dev(y=(y + 2) % 4)
    mate_z = zl + 1 - 2 * zlo
    mate, other_same, other_diff = dev(zl=mate_z), dev(zl=(zl + 2) % 4), dev(zl=(mate_z + 2) % 4)
    sibling = dev(k=1 - k)

    def remote(src, dst, ssem, rsem, target):
        return pltpu.make_async_remote_copy(
            src_ref=src, dst_ref=dst, send_sem=ssem, recv_sem=rsem, device_id=target, device_id_type=MESH
        )

    loads = [
        pltpu.make_async_copy(x_hbm, xd.at[0, k, zlo, 0], load_sem.at[0]),
        pltpu.make_async_copy(dy_hbm, xd.at[0, k, zlo, 1], load_sem.at[1]),
        pltpu.make_async_copy(wg_hbm, wg, load_sem.at[2]),
        pltpu.make_async_copy(wu_hbm, wu, load_sem.at[3]),
        pltpu.make_async_copy(wd_hbm, wd, load_sem.at[4]),
    ]
    for load in loads:
        load.start()

    barrier = pltpu.get_barrier_semaphore()
    others = (up, down, partner, yp, ym, yf, mate, other_same, other_diff, sibling)
    for other in others:
        pl.semaphore_signal(barrier, inc=1, device_id=other, device_id_type=MESH)
    loads[0].wait()
    loads[1].wait()
    pl.semaphore_wait(barrier, len(others))

    mine = xd.at[0, k, zlo]
    z_gather = [
        remote(mine, xd.at[0, k, zlo], p1_send.at[0], p1_recv.at[0], mate),
        remote(mine, xd.at[7, k, zlo], p1_send.at[1], p1_recv.at[1], other_same),
        remote(mine, xd.at[7, k, zlo], p1_send.at[2], p1_recv.at[2], other_diff),
    ]

    def to_sibling(c):
        return remote(xd.at[c, k], xd.at[c, k], sib_send.at[c], sib_recv.at[c], sibling)

    y_gather = [
        remote(xd.at[0, k], xd.at[2, k], y_send.at[0], y_recv.at[0], yp),
        remote(xd.at[0, k], xd.at[1, k], y_send.at[1], y_recv.at[1], ym),
        remote(xd.at[7, k], xd.at[4, k], y_send.at[2], y_recv.at[2], yp),
        remote(xd.at[7, k], xd.at[3, k], y_send.at[3], y_recv.at[3], ym),
        remote(xd.at[2, k, 0], xd.at[5, k, 0], y_send.at[4], y_recv.at[4], yp),
        remote(xd.at[1, k, 1], xd.at[5, k, 1], y_send.at[5], y_recv.at[5], ym),
        remote(xd.at[4, k, 0], xd.at[6, k, 0], y_send.at[6], y_recv.at[6], yp),
        remote(xd.at[3, k, 1], xd.at[6, k, 1], y_send.at[7], y_recv.at[7], ym),
    ]

    def gather_step(step):
        if step == 0:
            z_gather[0].wait_recv()
            y_gather[0].start()
            y_gather[1].start()
            to_sibling(0).start()
        elif step == 1:
            z_gather[1].wait_recv()
            z_gather[2].wait_recv()
            y_gather[2].start()
            y_gather[3].start()
            to_sibling(7).start()
        elif step == 2:
            y_gather[0].wait_recv()
            y_gather[1].wait_recv()
            y_gather[4].start()
            y_gather[5].start()
            to_sibling(1).start()
            to_sibling(2).start()
        elif step == 3:
            y_gather[2].wait_recv()
            y_gather[3].wait_recv()
            y_gather[6].start()
            y_gather[7].start()
            to_sibling(3).start()
            to_sibling(4).start()
        elif step == 4:
            y_gather[4].wait_recv()
            y_gather[5].wait_recv()
            to_sibling(5).start()
        elif step == 5:
            y_gather[6].wait_recv()
            y_gather[7].wait_recv()
            to_sibling(6).start()

    def copy(c, which):
        ends = {
            RELAY_LO: (s_far.at[c, :, lo], r_relay.at[c, :, lo], up),
            RELAY_HI: (s_far.at[c, :, hi], r_relay.at[c, :, hi], down),
            DIRECT_HI: (s_near.at[c, :, hi], r_near.at[c, :, hi], up),
            DIRECT_LO: (s_near.at[c, :, lo], r_near.at[c, :, lo], down),
            SUM_LO: (s_sum.at[c, :, lo], r_sum.at[c, :, lo], up),
            SUM_HI: (s_sum.at[c, :, hi], r_sum.at[c, :, hi], down),
            ZSUM: (s_z.at[c], r_z.at[c], partner),
            OWN_UP_LO: (grads.at[c, x, :, lo], grads.at[c, x, :, lo], up),
            OWN_UP_HI: (grads.at[c, x, :, hi], grads.at[c, x, :, hi], up),
            OWN_DN_HI: (grads.at[c, x, :, hi], grads.at[c, x, :, hi], down),
            OWN_DN_LO: (grads.at[c, x, :, lo], grads.at[c, x, :, lo], down),
            FWD_LO: (grads.at[c, xm, :, lo], grads.at[c, xm, :, lo], up),
            FWD_HI: (grads.at[c, xp, :, hi], grads.at[c, xp, :, hi], down),
        }
        src, dst, target = ends[which]
        return remote(src, dst, send.at[c, which], recv.at[c, which], target)

    def stage_a(c):
        to_sibling(c).wait_recv()
        xs = xd[c, :, :, 0].reshape(64, -1)
        ds = xd[c, :, :, 1].reshape(64, -1)
        gate = jnp.dot(xs, wg[...], preferred_element_type=F32)
        part[c, :, :, 0:ff] = gate.reshape(4, 16, ff)
        upper = jnp.dot(xs, wu[...], preferred_element_type=F32)
        part[c, :, :, ff : 2 * ff] = upper.reshape(4, 16, ff)
        hgrad = lax.dot_general(ds, wd[...], NT, preferred_element_type=F32)
        part[c, :, :, 2 * ff :] = hgrad.reshape(4, 16, ff)
        s_far[c] = part[c, xf].astype(BF16)
        copy(c, RELAY_LO).start()
        copy(c, RELAY_HI).start()
        s_near[c, :, hi] = part[c, xp, :, hi].astype(BF16)
        s_near[c, :, lo] = part[c, xm, :, lo].astype(BF16)
        copy(c, DIRECT_HI).start()
        copy(c, DIRECT_LO).start()

    def stage_b(c):
        copy(c, RELAY_LO).wait_recv()
        s_sum[c, :, lo] = (part[c, xp, :, lo] + r_relay[c, :, lo].astype(F32)).astype(BF16)
        copy(c, SUM_LO).start()
        copy(c, RELAY_HI).wait_recv()
        s_sum[c, :, hi] = (part[c, xm, :, hi] + r_relay[c, :, hi].astype(F32)).astype(BF16)
        copy(c, SUM_HI).start()

    def stage_c(c):
        for which in (DIRECT_HI, DIRECT_LO, SUM_LO, SUM_HI):
            copy(c, which).wait_recv()
        total = part[c, x] + r_near[c].astype(F32) + r_sum[c].astype(F32)
        part[c, x] = total
        s_z[c] = total.astype(BF16)
        copy(c, ZSUM).start()

    def stage_d(c):
        copy(c, ZSUM).wait_recv()
        gate = part[c, x, :, 0:ff] + r_z[c, :, 0:ff].astype(F32)
        upper = part[c, x, :, ff : 2 * ff] + r_z[c, :, ff : 2 * ff].astype(F32)
        hgrad = part[c, x, :, 2 * ff :] + r_z[c, :, 2 * ff :].astype(F32)
        sigm = 1.0 / (1.0 + jnp.exp(-gate))
        act = gate * sigm
        grads[c, x, :, 0:ff] = (act * upper).astype(BF16)
        grads[c, x, :, ff : 2 * ff] = (hgrad * upper * sigm * (1.0 + gate * (1.0 - sigm))).astype(BF16)
        grads[c, x, :, 2 * ff :] = (hgrad * act).astype(BF16)
        for which in (OWN_UP_LO, OWN_DN_HI, OWN_UP_HI, OWN_DN_LO):
            copy(c, which).start()

    def stage_f(c):
        copy(c, OWN_UP_LO).wait_recv()
        copy(c, FWD_LO).start()
        copy(c, OWN_DN_HI).wait_recv()
        copy(c, FWD_HI).start()

    def outs(c):
        return [
            pltpu.make_async_copy(grads.at[c, :, :, pl.ds(0, ff)], h_hbm.at[c], out_sem.at[c, 0]),
            pltpu.make_async_copy(grads.at[c, :, :, pl.ds(ff, ff)], gg_hbm.at[c], out_sem.at[c, 1]),
            pltpu.make_async_copy(grads.at[c, :, :, pl.ds(2 * ff, ff)], ug_hbm.at[c], out_sem.at[c, 2]),
            pltpu.make_async_copy(xd.at[c, :, :, 0], xo_hbm.at[c], out_sem.at[c, 3]),
            pltpu.make_async_copy(xd.at[c, :, :, 1], do_hbm.at[c], out_sem.at[c, 4]),
        ]

    def ig_to_sibling(c):
        return remote(ig_part.at[c, 1 - k], ig_sib.at[c], ig_sib_send.at[c], ig_sib_recv.at[c], sibling)

    def stage_g(c):
        for which in (OWN_UP_HI, OWN_DN_LO, FWD_LO, FWD_HI):
            copy(c, which).wait_recv()
        for out in outs(c):
            out.start()
        gg = grads[c, :, :, ff : 2 * ff].reshape(64, ff)
        ug = grads[c, :, :, 2 * ff :].reshape(64, ff)
        total = lax.dot_general(gg, wg[...], NT, preferred_element_type=F32)
        total = total + lax.dot_general(ug, wu[...], NT, preferred_element_type=F32)
        ig_part[c] = total.reshape(2, 2, 16, -1)
        ig_to_sibling(c).start()

    def ig_to_y(c):
        dy, other = CHUNK_OF[c]
        slot = (dy - 1) * 2 + other
        target = {1: yp, 2: yf, 3: ym}[dy]
        return remote(ig_ysend.at[slot], ig_yrecv.at[slot], ig_y_send.at[slot], ig_y_recv.at[slot], target)

    def stage_h(c):
        ig_to_sibling(c).wait_recv()
        total = ig_part[c, k] + ig_sib[c]
        ig_part[c, k] = total
        for i in range(1, 7):
            dy, other = CHUNK_OF[i]

            @pl.when(c == i)
            def _(i=i, slot=(dy - 1) * 2 + other):
                ig_ysend[slot] = total
                ig_to_y(i).start()

    def own(other, block):
        total = ig_part[7 * other, k, block]
        for dy in range(3):
            total = total + ig_yrecv[dy * 2 + other, block]
        return total

    to_mate = remote(ig_msend, ig_mrecv, ig_z_send.at[2], ig_z_recv.at[2], mate)

    def send_to_mate():
        for i in (1, 2, 5):
            ig_to_y(i).wait_recv()
        ig_msend[...] = own(0, 1 - zlo)
        to_mate.start()

    for z_copy in z_gather:
        z_copy.start()
    for load in loads[2:]:
        load.wait()

    @pl.loop(0, CHUNKS + LAG_H)
    def _(s):
        for step in range(6):
            at = 0 if step == 0 else step - 1

            def run(step=step):
                gather_step(step)

            if step == 1:
                continue
            pl.when(s == at)(run)

        @pl.when(s < CHUNKS)
        def _():
            stage_a(s)

        @pl.when(s == 0)
        def _():
            gather_step(1)

        pl.when(s == CHUNKS + LAG_H - 1)(send_to_mate)

        for stage, lag in (
            (stage_b, LAG_B), (stage_c, LAG_C), (stage_d, LAG_D), (stage_f, LAG_F), (stage_g, LAG_G), (stage_h, LAG_H),
        ):

            @pl.when((s >= lag) & (s < CHUNKS + lag))
            def _(stage=stage, lag=lag):
                stage(s - lag)

    for i in (3, 4, 6):
        ig_to_y(i).wait_recv()
    z_scatter = []
    for i, (block, target) in enumerate(((zlo, other_same), (1 - zlo, other_diff))):
        ig_zsend[i] = own(1, block).astype(BF16)
        z_copy = remote(ig_zsend.at[i], ig_zrecv.at[i], ig_z_send.at[i], ig_z_recv.at[i], target)
        z_copy.start()
        z_scatter.append(z_copy)
    to_mate.wait_recv()
    total = own(0, zlo) + ig_mrecv[...]
    for i in range(2):
        z_scatter[i].wait_recv()
        total = total + ig_zrecv[i].astype(F32)
    ig_ref[...] = total.astype(BF16)

    for z_copy in z_gather + z_scatter + y_gather + [to_mate]:
        z_copy.wait_send()
    for i in range(1, 7):
        ig_to_y(i).wait_send()

    @pl.loop(0, CHUNKS)
    def _(c):
        for which in range(PER_CHUNK):
            copy(c, which).wait_send()
        to_sibling(c).wait_send()
        ig_to_sibling(c).wait_send()
        for out in outs(c):
            out.wait()


def body(inputs, out_grad, gate_weight, up_weight, down_weight):
    feats, ff = gate_weight.shape
    blocks = (CHUNKS, 4, 16)
    anywhere = pl.BlockSpec(memory_space=pl.ANY)
    slot = (CHUNKS, 16, 3 * ff)
    dma = pltpu.SemaphoreType.DMA
    input_grad, x_all, d_all, hidden, gate_grad, up_grad = pl.pallas_call(
        comm_kernel,
        out_shape=[
            jax.ShapeDtypeStruct((16, feats), BF16),
            jax.ShapeDtypeStruct((CHUNKS, 2, 2, 16, feats), BF16),
            jax.ShapeDtypeStruct((CHUNKS, 2, 2, 16, feats), BF16),
            jax.ShapeDtypeStruct(blocks + (ff,), BF16),
            jax.ShapeDtypeStruct(blocks + (ff,), BF16),
            jax.ShapeDtypeStruct(blocks + (ff,), BF16),
        ],
        in_specs=[anywhere] * 5,
        out_specs=[pl.BlockSpec(memory_space=pltpu.VMEM)] + [anywhere] * 5,
        scratch_shapes=[
            pltpu.VMEM((CHUNKS, 2, 2, 2, 16, feats), BF16),
            pltpu.VMEM((feats, ff), BF16),
            pltpu.VMEM((feats, ff), BF16),
            pltpu.VMEM((ff, feats), BF16),
            pltpu.VMEM((CHUNKS, 4, 16, 3 * ff), F32),
            pltpu.VMEM(slot, BF16),
            pltpu.VMEM(slot, BF16),
            pltpu.VMEM(slot, BF16),
            pltpu.VMEM(slot, BF16),
            pltpu.VMEM(slot, BF16),
            pltpu.VMEM(slot, BF16),
            pltpu.VMEM(slot, BF16),
            pltpu.VMEM(slot, BF16),
            pltpu.VMEM(blocks + (3 * ff,), BF16),
            pltpu.VMEM((CHUNKS, 2, 2, 16, feats), F32),
            pltpu.VMEM((CHUNKS, 2, 16, feats), F32),
            pltpu.VMEM((6, 2, 16, feats), F32),
            pltpu.VMEM((6, 2, 16, feats), F32),
            pltpu.VMEM((16, feats), F32),
            pltpu.VMEM((16, feats), F32),
            pltpu.VMEM((2, 16, feats), BF16),
            pltpu.VMEM((2, 16, feats), BF16),
            dma((5,)),
            dma((CHUNKS, PER_CHUNK)),
            dma((CHUNKS, PER_CHUNK)),
            dma((3,)),
            dma((3,)),
            dma((CHUNKS,)),
            dma((CHUNKS,)),
            dma((8,)),
            dma((8,)),
            dma((CHUNKS,)),
            dma((CHUNKS,)),
            dma((6,)),
            dma((6,)),
            dma((3,)),
            dma((3,)),
            dma((CHUNKS, 5)),
        ],
        compiler_params=pltpu.CompilerParams(
            collective_id=0, has_side_effects=True, vmem_limit_bytes=48 * 2**20
        ),
        name="comm",
    )(inputs, out_grad, gate_weight, up_weight, down_weight)

    def flat(a):
        return a.reshape(-1, a.shape[-1])

    def weight_grad(a, b):
        return lax.dot_general(
            flat(a), flat(b), (((0,), (0,)), ((), ())), preferred_element_type=F32
        ).astype(BF16)

    return (
        input_grad,
        weight_grad(x_all, gate_grad),
        weight_grad(x_all, up_grad),
        weight_grad(hidden, d_all),
    )


def solution(mesh):
    return jax.shard_map(
        body,
        mesh=mesh,
        in_specs=(P("col", "row"), P("col", "row"), P("row", "col"), P("row", "col"), P("col", "row")),
        out_specs=(P("col", "row"), P("row", "col"), P("row", "col"), P("col", "row")),
        check_vma=False,
    )
```

time: 688 us -> 94.7 us (0.14)
  waiting for transfers between devices: 482 us -> 0 us
  blocking collectives: 150 us -> 0 us
  Pallas kernels: 0 us -> 84.3 us
  matrix products: 24.9 us -> 7.39 us
  between operations: 14.1 us -> 0.65 us
  local copies, waits for them, and re-layouts: 9.76 us -> 2.12 us
    reduce_scatter x4 -> x0, waiting for transfers between devices: 364 us -> none  [the longest x1 93 us: body(): lax.psum_scatter(gate_part, 'row', scatter_dimension=0, tiled=True)]
    all_gather x3 -> x0, blocking collectives: 150 us -> none  [the longest x1 52.9 us: body(): lax.all_gather(hidden, 'row', axis=0, tiled=True)]
    all_gather x2 -> x0, waiting for transfers between devices: 116 us -> none  [the longest x1 64.3 us: body(): lax.all_gather(inputs, 'col', axis=0, tiled=True)]
    pallas_call x0 -> x1, Pallas kernels: none -> 84.3 us  [body(): pl.pallas_call(comm_kernel, out_shape=[jax.ShapeDtypeStruct((16, feats),...]
    dot_general x8 -> x3, matrix products: 24.9 us -> 7.39 us  [weight_grad(): lax.dot_general(flat(a), flat(b), (((0,), (0,)), ((), ())), preferred_ele...]
    unnamed x12 -> x5, local copies, waits for them, and re-layouts: 9.76 us -> 2.12 us
  transfers between devices with their start and end apart: 6 -> 0, of which waited for: 6 -> 0; matrix products, arithmetic and copies ran while one was open for 4% -> 0% of each run, Pallas kernels for 0% -> 0%
where the time goes in v1:
time: 94.7 us; the launch traced here: 94.5 us
  Pallas kernels  84.3 us (89%)
  matrix products  7.39 us (8%)
  local copies, waits for them, and re-layouts  2.12 us (2%)
    pallas_call x1, Pallas kernels, body(): pl.pallas_call(comm_kernel, out_shape=[jax.ShapeDtypeStruct((16, feats),...  84.3 us
    dot_general x3, matrix products, weight_grad(): lax.dot_general(flat(a), flat(b), (((0,), (0,)), ((), ())), preferred_ele...  7.39 us
    unnamed x5, local copies, waits for them, and re-layouts  2.12 us

profile of v1, /device:TPU:1, one launch (start us, length us, event | category | flops | bytes accessed | tf_op | source)
XLA Modules:
  0.0 94.5 jit_solution(7719963486511871947)
XLA Ops:
  0.6 0.0 copy-start
  0.6 0.7 copy-done
  1.4 0.0 copy-start.1
  1.4 0.8 copy-done.1
  2.1 84.3 %comm.1 = (bf16[16,1024]{1,0:T(8,128)(2,1)S(1)}, bf16[8,2,2,16,1024]{4,3,2,1,0:T(8,128)(2,1)S(1)}, bf16[8,2,2,16,1024]{4,3,2,1,0:T(8,128)(2,1)S(1)}, bf16[8,4,16...) custom-call(bf16[16,1024]{1,0:T(8,128)(2,1)S(1)} %copy-done, ...), custom_call_target="tpu_custom_call" | custom-call | tf_op jit(solution)/shard_map/comm/pallas_call | solution.py:329
  86.5 2.5 %convolution_convert_fusion.1 = bf16[1024,896]{1,0:T(8,128)(2,1)} fusion(bf16[512,1024]{1,0:T(8,128)(2,1)S(1)} %bitcast.12, bf16[512,896]{1,0:T(8,128)(2,1)S(1)} %bitcast.16), kind=kOutput, calls=%fused_computation.1 | convolution fusion | flops 940441600 | bytes 3801088 | tf_op jit(solution)/shard_map/dot_general | solution.py:391
  89.0 2.5 %convolution_convert_fusion.2 = bf16[1024,896]{1,0:T(8,128)(2,1)} fusion(bf16[512,1024]{1,0:T(8,128)(2,1)S(1)} %bitcast.13, bf16[512,896]{1,0:T(8,128)(2,1)S(1)} %bitcast.15), kind=kOutput, calls=%fused_computation.2 | convolution fusion | flops 940441600 | bytes 3801088 | tf_op jit(solution)/shard_map/dot_general | solution.py:391
  91.5 2.4 %convolution_convert_fusion = bf16[896,1024]{1,0:T(8,128)(2,1)} fusion(bf16[512,896]{1,0:T(8,128)(2,1)S(1)} %bitcast.14, bf16[512,1024]{1,0:T(8,128)(2,1)S(1)} %bitcast.11), kind=kOutput, calls=%fused_computation | convolution fusion | flops 940441600 | bytes 3801088 | tf_op jit(solution)/shard_map/dot_general | solution.py:391
  93.9 0.6 copy.10
Async XLA Ops:
  0.6 0.8 copy-start
  1.4 0.8 copy-start.1

commit v2 on v1

--- a/solution.py
+++ b/solution.py
@@ -11,21 +11,43 @@
 
 CHUNKS = 8
 CHUNK_OF = ((0, 0), (1, 0), (3, 0), (1, 1), (3, 1), (2, 0), (2, 1), (0, 1))
-LAG_B, LAG_C, LAG_D, LAG_F, LAG_G, LAG_H = 1, 2, 5, 6, 7, 8
+
+BEFORE_A = (
+    ("g0",),
+    ("g2", "b0", "B0", "g1",),
+    (),
+    ("P", "C0", "g4", "b1", "B1", "g3", "b2", "B2",),
+    (),
+    ("C1", "C2", "g5",),
+    ("b3", "B3",),
+    ("b4", "B4", "D0",),
+)
+BEFORE_G = (
+    ("b5", "B5", "C3", "b6", "B6", "D1", "C4", "f0", "F0", "D2", "b7", "B7", "C5", "D3", "C6", "f1", "F1",),
+    ("f2", "F2", "D4", "H0", "C7", "f3", "F3", "D5",),
+    (),
+    ("f4", "F4", "H1", "D6", "H2",),
+    ("f5", "F5", "H3", "D7", "f6",),
+    ("F6", "H4", "f7",),
+    ("F7", "H5",),
+    (),
+)
+LAST = ("H6", "M", "H7",)
 
 RELAY_LO, RELAY_HI, DIRECT_HI, DIRECT_LO, SUM_LO, SUM_HI, ZSUM = range(7)
 OWN_UP_LO, OWN_UP_HI, OWN_DN_HI, OWN_DN_LO, FWD_LO, FWD_HI = range(7, 13)
 PER_CHUNK = 13
 NT = (((1,), (1,)), ((), ()))
+TN = (((0,), (0,)), ((), ()))
 
 
 def comm_kernel(
     x_hbm, dy_hbm, wg_hbm, wu_hbm, wd_hbm,
-    ig_ref, xo_hbm, do_hbm, h_hbm, gg_hbm, ug_hbm,
+    own_ref, other_ref, xo_hbm, do_hbm, h_hbm, gg_hbm, ug_hbm,
     xd, wg, wu, wd, part, s_far, s_near, s_sum, s_z, r_relay, r_near, r_sum, r_z, grads,
-    ig_part, ig_sib, ig_ysend, ig_yrecv, ig_msend, ig_mrecv, ig_zsend, ig_zrecv,
+    ig_part, ig_sib, ig_ysend, ig_yrecv, ig_msend, ig_mrecv,
     load_sem, send, recv, p1_send, p1_recv, sib_send, sib_recv, y_send, y_recv,
-    ig_sib_send, ig_sib_recv, ig_y_send, ig_y_recv, ig_z_send, ig_z_recv, out_sem,
+    ig_sib_send, ig_sib_recv, ig_y_send, ig_y_recv, ig_z_send, ig_z_recv, out_sem, here,
 ):
     ff = wg.shape[1]
     width = 3 * ff
@@ -47,6 +69,8 @@
     mate_z = zl + 1 - 2 * zlo
     mate, other_same, other_diff = dev(zl=mate_z), dev(zl=(zl + 2) % 4), dev(zl=(mate_z + 2) % 4)
     sibling = dev(k=1 - k)
+    zu, zd = (zh * 4 + zl + 1) % 8, (zh * 4 + zl + 7) % 8
+    zp, zm = dev(zh=zu // 4, zl=zu % 4), dev(zh=zd // 4, zl=zd % 4)
 
     def remote(src, dst, ssem, rsem, target):
         return pltpu.make_async_remote_copy(
@@ -64,12 +88,18 @@
         load.start()
 
     barrier = pltpu.get_barrier_semaphore()
-    others = (up, down, partner, yp, ym, yf, mate, other_same, other_diff, sibling)
-    for other in others:
+    near = (up, down, yp, ym, zp, zm, sibling)
+    for other in near:
         pl.semaphore_signal(barrier, inc=1, device_id=other, device_id_type=MESH)
     loads[0].wait()
     loads[1].wait()
-    pl.semaphore_wait(barrier, len(others))
+    pl.semaphore_wait(barrier, len(near))
+
+    def tell(which, target):
+        pl.semaphore_signal(here.at[which], inc=1, device_id=target, device_id_type=MESH)
+
+    def told(which):
+        pl.semaphore_wait(here.at[which], 1)
 
     mine = xd.at[0, k, zlo]
     z_gather = [
@@ -164,10 +194,12 @@
         copy(c, DIRECT_HI).start()
         copy(c, DIRECT_LO).start()
 
-    def stage_b(c):
+    def stage_b_lo(c):
         copy(c, RELAY_LO).wait_recv()
         s_sum[c, :, lo] = (part[c, xp, :, lo] + r_relay[c, :, lo].astype(F32)).astype(BF16)
         copy(c, SUM_LO).start()
+
+    def stage_b_hi(c):
         copy(c, RELAY_HI).wait_recv()
         s_sum[c, :, hi] = (part[c, xm, :, hi] + r_relay[c, :, hi].astype(F32)).astype(BF16)
         copy(c, SUM_HI).start()
@@ -193,9 +225,11 @@
         for which in (OWN_UP_LO, OWN_DN_HI, OWN_UP_HI, OWN_DN_LO):
             copy(c, which).start()
 
-    def stage_f(c):
+    def stage_f_lo(c):
         copy(c, OWN_UP_LO).wait_recv()
         copy(c, FWD_LO).start()
+
+    def stage_f_hi(c):
         copy(c, OWN_DN_HI).wait_recv()
         copy(c, FWD_HI).start()
 
@@ -232,14 +266,14 @@
     def stage_h(c):
         ig_to_sibling(c).wait_recv()
         total = ig_part[c, k] + ig_sib[c]
-        ig_part[c, k] = total
-        for i in range(1, 7):
-            dy, other = CHUNK_OF[i]
-
-            @pl.when(c == i)
-            def _(i=i, slot=(dy - 1) * 2 + other):
-                ig_ysend[slot] = total
-                ig_to_y(i).start()
+        dy, other = CHUNK_OF[c]
+        if dy == 0:
+            ig_part[c, k] = total
+        else:
+            ig_ysend[(dy - 1) * 2 + other] = total
+            if c == 5:
+                told(5)
+            ig_to_y(c).start()
 
     def own(other, block):
         total = ig_part[7 * other, k, block]
@@ -247,7 +281,7 @@
             total = total + ig_yrecv[dy * 2 + other, block]
         return total
 
-    to_mate = remote(ig_msend, ig_mrecv, ig_z_send.at[2], ig_z_recv.at[2], mate)
+    to_mate = remote(ig_msend, ig_mrecv, ig_z_send, ig_z_recv, mate)
 
     def send_to_mate():
         for i in (1, 2, 5):
@@ -255,57 +289,57 @@
         ig_msend[...] = own(0, 1 - zlo)
         to_mate.start()
 
-    for z_copy in z_gather:
-        z_copy.start()
+    z_gather[0].start()
+    tell(0, zm)
+    tell(1, zp)
+    tell(5, ym)
+    told(0)
+    told(1)
+    tell(2, zm)
+    tell(3, zp)
+    told(2)
+    told(3)
+    tell(4, zm)
+    z_gather[1].start()
+    z_gather[2].start()
     for load in loads[2:]:
         load.wait()
 
-    @pl.loop(0, CHUNKS + LAG_H)
+    steps = {
+        "g": gather_step, "b": stage_b_lo, "B": stage_b_hi, "C": stage_c, "D": stage_d,
+        "f": stage_f_lo, "F": stage_f_hi, "H": stage_h,
+    }
+
+    def run(names):
+        for name in names:
+            if name == "M":
+                send_to_mate()
+            elif name == "P":
+                told(4)
+            else:
+                steps[name[0]](int(name[1]))
+
+    @pl.loop(0, CHUNKS)
     def _(s):
-        for step in range(6):
-            at = 0 if step == 0 else step - 1
-
-            def run(step=step):
-                gather_step(step)
-
-            if step == 1:
-                continue
-            pl.when(s == at)(run)
-
-        @pl.when(s < CHUNKS)
-        def _():
-            stage_a(s)
-
-        @pl.when(s == 0)
-        def _():
-            gather_step(1)
-
-        pl.when(s == CHUNKS + LAG_H - 1)(send_to_mate)
-
-        for stage, lag in (
-            (stage_b, LAG_B), (stage_c, LAG_C), (stage_d, LAG_D), (stage_f, LAG_F), (stage_g, LAG_G), (stage_h, LAG_H),
-        ):
-
-            @pl.when((s >= lag) & (s < CHUNKS + lag))
-            def _(stage=stage, lag=lag):
-                stage(s - lag)
-
+        for i in range(CHUNKS):
+            pl.when(s == i)(lambda i=i: run(BEFORE_A[i]))
+        stage_a(s)
+
+    @pl.loop(0, CHUNKS)
+    def _(s):
+        for i in range(CHUNKS):
+            pl.when(s == i)(lambda i=i: run(BEFORE_G[i]))
+        stage_g(s)
+
+    run(LAST)
     for i in (3, 4, 6):
         ig_to_y(i).wait_recv()
-    z_scatter = []
-    for i, (block, target) in enumerate(((zlo, other_same), (1 - zlo, other_diff))):
-        ig_zsend[i] = own(1, block).astype(BF16)
-        z_copy = remote(ig_zsend.at[i], ig_zrecv.at[i], ig_z_send.at[i], ig_z_recv.at[i], target)
-        z_copy.start()
-        z_scatter.append(z_copy)
+    other_ref[0] = own(1, zlo)
+    other_ref[1] = own(1, 1 - zlo)
     to_mate.wait_recv()
-    total = own(0, zlo) + ig_mrecv[...]
-    for i in range(2):
-        z_scatter[i].wait_recv()
-        total = total + ig_zrecv[i].astype(F32)
-    ig_ref[...] = total.astype(BF16)
-
-    for z_copy in z_gather + z_scatter + y_gather + [to_mate]:
+    own_ref[...] = own(0, zlo) + ig_mrecv[...]
+
+    for z_copy in z_gather + y_gather + [to_mate]:
         z_copy.wait_send()
     for i in range(1, 7):
         ig_to_y(i).wait_send()
@@ -320,16 +354,38 @@
             out.wait()
 
 
+def weight_grad_kernel(
+    xv, dv, hv, gv, uv, gate_hbm, up_hbm, down_hbm, gate_up, down, out_sem,
+):
+    stores = []
+
+    def product(which, lhs, rhs, buffer, target):
+        rows = lhs.shape[1]
+        for i in range(0, rows, 256):
+            part = pl.ds(i, min(256, rows - i))
+            buffer[part] = lax.dot_general(lhs[:, part], rhs[...], TN, preferred_element_type=F32).astype(BF16)
+            store = pltpu.make_async_copy(buffer.at[part], target.at[part], out_sem.at[which, i // 256])
+            store.start()
+            stores.append(store)
+
+    product(0, xv, gv, gate_up.at[0], gate_hbm)
+    product(1, xv, uv, gate_up.at[1], up_hbm)
+    product(2, hv, dv, down, down_hbm)
+    for store in stores:
+        store.wait()
+
+
 def body(inputs, out_grad, gate_weight, up_weight, down_weight):
     feats, ff = gate_weight.shape
     blocks = (CHUNKS, 4, 16)
-    anywhere = pl.BlockSpec(memory_space=pl.ANY)
+    anywhere = pl.BlockSpec(memory_space=pltpu.HBM)
     slot = (CHUNKS, 16, 3 * ff)
     dma = pltpu.SemaphoreType.DMA
-    input_grad, x_all, d_all, hidden, gate_grad, up_grad = pl.pallas_call(
+    own, other, x_all, d_all, hidden, gate_grad, up_grad = pl.pallas_call(
         comm_kernel,
         out_shape=[
-            jax.ShapeDtypeStruct((16, feats), BF16),
+            jax.ShapeDtypeStruct((16, feats), F32),
+            jax.ShapeDtypeStruct((2, 16, feats), F32),
             jax.ShapeDtypeStruct((CHUNKS, 2, 2, 16, feats), BF16),
             jax.ShapeDtypeStruct((CHUNKS, 2, 2, 16, feats), BF16),
             jax.ShapeDtypeStruct(blocks + (ff,), BF16),
@@ -337,7 +393,7 @@
             jax.ShapeDtypeStruct(blocks + (ff,), BF16),
         ],
         in_specs=[anywhere] * 5,
-        out_specs=[pl.BlockSpec(memory_space=pltpu.VMEM)] + [anywhere] * 5,
+        out_specs=[pl.BlockSpec(memory_space=pltpu.VMEM)] * 2 + [anywhere] * 5,
         scratch_shapes=[
             pltpu.VMEM((CHUNKS, 2, 2, 2, 16, feats), BF16),
             pltpu.VMEM((feats, ff), BF16),
@@ -359,8 +415,6 @@
             pltpu.VMEM((6, 2, 16, feats), F32),
             pltpu.VMEM((16, feats), F32),
             pltpu.VMEM((16, feats), F32),
-            pltpu.VMEM((2, 16, feats), BF16),
-            pltpu.VMEM((2, 16, feats), BF16),
             dma((5,)),
             dma((CHUNKS, PER_CHUNK)),
             dma((CHUNKS, PER_CHUNK)),
@@ -374,30 +428,52 @@
             dma((CHUNKS,)),
             dma((6,)),
             dma((6,)),
-            dma((3,)),
-            dma((3,)),
+            dma(()),
+            dma(()),
             dma((CHUNKS, 5)),
+            pltpu.SemaphoreType.REGULAR((6,)),
         ],
         compiler_params=pltpu.CompilerParams(
             collective_id=0, has_side_effects=True, vmem_limit_bytes=48 * 2**20
         ),
         name="comm",
-    )(inputs, out_grad, gate_weight, up_weight, down_weight)
+    )(*(pltpu.with_memory_space_constraint(a, pltpu.HBM) for a in (inputs, out_grad)), gate_weight, up_weight, down_weight)
+
+    def far(i, col):
+        z_lo = col // 8
+        target = (z_lo + 2) % 4 if i == 0 else (z_lo + 3 - 2 * (z_lo % 2)) % 4
+        return (col, target * 8 + col % 8)
+
+    from_far = [lax.ppermute(other[i], "col", [far(i, col) for col in range(32)]) for i in range(2)]
 
     def flat(a):
         return a.reshape(-1, a.shape[-1])
 
-    def weight_grad(a, b):
-        return lax.dot_general(
-            flat(a), flat(b), (((0,), (0,)), ((), ())), preferred_element_type=F32
-        ).astype(BF16)
-
-    return (
-        input_grad,
-        weight_grad(x_all, gate_grad),
-        weight_grad(x_all, up_grad),
-        weight_grad(hidden, d_all),
-    )
+    tokens = flat(x_all).shape[0]
+    gate_weight_grad, up_weight_grad, down_weight_grad = pl.pallas_call(
+        weight_grad_kernel,
+        out_shape=[
+            jax.ShapeDtypeStruct((feats, ff), BF16),
+            jax.ShapeDtypeStruct((feats, ff), BF16),
+            jax.ShapeDtypeStruct((ff, feats), BF16),
+        ],
+        in_specs=[pl.BlockSpec(memory_space=pltpu.VMEM)] * 5,
+        out_specs=[anywhere] * 3,
+        scratch_shapes=[
+            pltpu.VMEM((2, feats, ff), BF16),
+            pltpu.VMEM((ff, feats), BF16),
+            dma((3, 4)),
+        ],
+        compiler_params=pltpu.CompilerParams(vmem_limit_bytes=32 * 2**20),
+        cost_estimate=pl.CostEstimate(
+            flops=6 * tokens * feats * ff,
+            bytes_accessed=6 * feats * ff + 2 * tokens * (2 * feats + 3 * ff),
+            transcendentals=0,
+        ),
+        name="weight_grads",
+    )(flat(x_all), flat(d_all), flat(hidden), flat(gate_grad), flat(up_grad))
+    input_grad = (own + from_far[0] + from_far[1]).astype(BF16)
+    return input_grad, gate_weight_grad, up_weight_grad, down_weight_grad
 
 
 def solution(mesh):

time: 94.7 us -> 86.3 us (0.911)
  matrix products: 7.39 us -> 0 us
  starting transfers between devices: 0 us -> 3.27 us
  Pallas kernels: 84.3 us -> 81.6 us
  local copies, waits for them, and re-layouts: 2.12 us -> 0.01 us
    dot_general x3 -> x0, matrix products: 7.39 us -> none  [weight_grad(): lax.dot_general(flat(a), flat(b), (((0,), (0,)), ((), ())), preferred_ele...]
    pallas_call x1, Pallas kernels: 84.3 us -> 77.5 us  [body(): pl.pallas_call(comm_kernel, out_shape=[jax.ShapeDtypeStruct((16, feats),...]
    pallas_call x0 -> x1, Pallas kernels: none -> 4.16 us  [body(): pl.pallas_call(weight_grad_kernel, out_shape=[jax.ShapeDtypeStruct((feats...]
    ppermute x0 -> x2, starting transfers between devices: none -> 3.27 us  [body(): lax.ppermute(other[i], 'col', [far(i, col) for col in range(32)])]
    unnamed x5 -> x0, local copies, waits for them, and re-layouts: 2.12 us -> none
  transfers between devices with their start and end apart: 0 -> 2, of which waited for: 0 -> 0; matrix products, arithmetic and copies ran while one was open for 0% -> 0% of each run, Pallas kernels for 0% -> 5%
where the time goes in v2:
time: 86.3 us; the launch traced here: 86.2 us
  Pallas kernels  81.6 us (95%)
  starting transfers between devices  3.27 us (4%)
    pallas_call x1, Pallas kernels, body(): pl.pallas_call(comm_kernel, out_shape=[jax.ShapeDtypeStruct((16, feats),...  77.5 us
    pallas_call x1, Pallas kernels, body(): pl.pallas_call(weight_grad_kernel, out_shape=[jax.ShapeDtypeStruct((feats...  4.16 us
    ppermute x2, starting transfers between devices, body(): lax.ppermute(other[i], 'col', [far(i, col) for col in range(32)])  3.27 us
  transfers between devices with their start and end apart: 2, of which 0 were waited for; matrix products, arithmetic and copies ran while one was open for 0% of the time, Pallas kernels for 5%

profile of v2, /device:TPU:1, one launch (start us, length us, event | category | flops | bytes accessed | tf_op | source)
XLA Modules:
  0.0 86.2 jit_solution(391246782739315946)
XLA Ops:
  0.6 77.5 %comm.1 = (f32[16,1024]{1,0:T(8,128)S(1)}, f32[2,16,1024]{2,1,0:T(8,128)S(1)}, bf16[8,2,2,16,1024]{4,3,2,1,0:T(8,128)(2,1)S(1)}, bf16[8,2,2,16,1024]{4,3,2,1,0:T...) custom-call(bf16[16,1024]{1,0:T(8,128)(2,1)} %x_hbm.1, ...), custom_call_target="tpu_custom_call" | custom-call | tf_op jit(solution)/shard_map/comm/pallas_call | solution.py:384
  78.1 1.7 %collective-permute-start = (f32[16,1024]{1,0:T(8,128)S(1)}, f32[16,1024]{1,0:T(8,128)S(1)}, u32[]{:S(2)}, u32[]{:S(2)}) collective-permute-start(f32[16,1024]{1,0:T(8,128)S(1)} %get-tuple-element.24), channel_id=1, source_target_pairs={{0,16},{1,17},{2,18},{3,19},{4,20},{5,21},{6,22},{7,23},{8,24},{9,... | collective-permute-start | bytes 196616 | tf_op jit(solution)/shard_map/ppermute | solution.py:447
  79.8 1.6 %collective-permute-start.1 = (f32[16,1024]{1,0:T(8,128)S(1)}, f32[16,1024]{1,0:T(8,128)S(1)}, u32[]{:S(2)}, u32[]{:S(2)}) collective-permute-start(f32[16,1024]{1,0:T(8,128)S(1)} %get-tuple-element.25), channel_id=1, source_target_pairs={{0,24},{1,25},{2,26},{3,27},{4,28},{5,29},{6,30},{7,31},{8,16},{9,... | collective-permute-start | bytes 196616 | tf_op jit(solution)/shard_map/ppermute | solution.py:447
  81.4 4.2 %weight_grads.1 = (bf16[1024,896]{1,0:T(8,128)(2,1)}, bf16[1024,896]{1,0:T(8,128)(2,1)}, bf16[896,1024]{1,0:T(8,128)(2,1)}) custom-call(bf16[512,1024]{1,0:T(8,128)(2,1)S(1)} %bitcast.9, bf16[512,1024]{1,0:T(8,128)(2,1)S(1)} %bitcast.10, bf16[512,896]{1,0:T(8,128)(2,1)S(1)} %bitcast.11, bf16[512,896]{1,0:T(8,128)(2,1)S(1)} %bitcast.12, ...), custom_call_target="tpu_custom_call" | custom-call | flops 2818572288 | bytes 10354688 | tf_op jit(solution)/shard_map/weight_grads/pallas_call | solution.py:453
  85.6 0.0 collective-permute-done
  85.6 0.0 collective-permute-done.1
  85.6 0.6 add_convert_fusion
  (1 shorter events, 0.0 us)
Async XLA Ops:
  78.1 7.4 %collective-permute-start = (f32[16,1024]{1,0:T(8,128)S(1)}, f32[16,1024]{1,0:T(8,128)S(1)}, u32[]{:S(2)}, u32[]{:S(2)}) collective-permute-start(f32[16,1024]{1,0:T(8,128)S(1)} %get-tuple-element.24), channel_id=1, source_target_pairs={{0,16},{1,17},{2,18},{3,19},{4,20},{5,21},{6,22},{7,23},{8,24},{9,... | collective-permute-start | bytes 196616 | tf_op jit(solution)/shard_map/ppermute | solution.py:447
  79.8 5.8 %collective-permute-start.1 = (f32[16,1024]{1,0:T(8,128)S(1)}, f32[16,1024]{1,0:T(8,128)S(1)}, u32[]{:S(2)}, u32[]{:S(2)}) collective-permute-start(f32[16,1024]{1,0:T(8,128)S(1)} %get-tuple-element.25), channel_id=1, source_target_pairs={{0,24},{1,25},{2,26},{3,27},{4,28},{5,29},{6,30},{7,31},{8,16},{9,... | collective-permute-start | bytes 196616 | tf_op jit(solution)/shard_map/ppermute | solution.py:447

commit v3 on v2

--- a/solution.py
+++ b/solution.py
@@ -30,9 +30,9 @@
     ("f5", "F5", "H3", "D7", "f6",),
     ("F6", "H4", "f7",),
     ("F7", "H5",),
-    (),
+    ("H6",),
 )
-LAST = ("H6", "M", "H7",)
+LAST = ("M", "H7",)
 
 RELAY_LO, RELAY_HI, DIRECT_HI, DIRECT_LO, SUM_LO, SUM_HI, ZSUM = range(7)
 OWN_UP_LO, OWN_UP_HI, OWN_DN_HI, OWN_DN_LO, FWD_LO, FWD_HI = range(7, 13)
@@ -305,6 +305,14 @@
     for load in loads[2:]:
         load.wait()
 
+    def drain(c):
+        for which in range(PER_CHUNK):
+            copy(c, which).wait_send()
+        to_sibling(c).wait_send()
+        ig_to_sibling(c).wait_send()
+        for out in outs(c):
+            out.wait()
+
     steps = {
         "g": gather_step, "b": stage_b_lo, "B": stage_b_hi, "C": stage_c, "D": stage_d,
         "f": stage_f_lo, "F": stage_f_hi, "H": stage_h,
@@ -329,6 +337,11 @@
     def _(s):
         for i in range(CHUNKS):
             pl.when(s == i)(lambda i=i: run(BEFORE_G[i]))
+
+        @pl.when(s >= 2)
+        def _():
+            drain(s - 2)
+
         stage_g(s)
 
     run(LAST)
@@ -344,14 +357,8 @@
     for i in range(1, 7):
         ig_to_y(i).wait_send()
 
-    @pl.loop(0, CHUNKS)
-    def _(c):
-        for which in range(PER_CHUNK):
-            copy(c, which).wait_send()
-        to_sibling(c).wait_send()
-        ig_to_sibling(c).wait_send()
-        for out in outs(c):
-            out.wait()
+    for c in (CHUNKS - 2, CHUNKS - 1):
+        drain(c)
 
 
 def weight_grad_kernel(

time: 86.3 us -> 85.6 us (level)
  no operation moved by 1% of the time
where the time goes in v3:
time: 85.6 us; the launch traced here: 85.3 us
  Pallas kernels  81.6 us (95%)
  starting transfers between devices  2.44 us (3%)
    pallas_call x1, Pallas kernels, body(): pl.pallas_call(comm_kernel, out_shape=[jax.ShapeDtypeStruct((16, feats),...  77.4 us
    pallas_call x1, Pallas kernels, body(): pl.pallas_call(weight_grad_kernel, out_shape=[jax.ShapeDtypeStruct((feats...  4.16 us
    ppermute x2, starting transfers between devices, body(): lax.ppermute(other[i], 'col', [far(i, col) for col in range(32)])  2.44 us
  transfers between devices with their start and end apart: 2, of which 0 were waited for; matrix products, arithmetic and copies ran while one was open for 0% of the time, Pallas kernels for 5%

profile of v3, /device:TPU:1, one launch (start us, length us, event | category | flops | bytes accessed | tf_op | source)
XLA Modules:
  0.0 85.3 jit_solution(10200983807016273099)
XLA Ops:
  0.6 77.4 %comm.1 = (f32[16,1024]{1,0:T(8,128)S(1)}, f32[2,16,1024]{2,1,0:T(8,128)S(1)}, bf16[8,2,2,16,1024]{4,3,2,1,0:T(8,128)(2,1)S(1)}, bf16[8,2,2,16,1024]{4,3,2,1,0:T...) custom-call(bf16[16,1024]{1,0:T(8,128)(2,1)} %x_hbm.1, ...), custom_call_target="tpu_custom_call" | custom-call | tf_op jit(solution)/shard_map/comm/pallas_call | solution.py:391
  78.1 0.8 collective-permute-start
  78.9 1.6 %collective-permute-start.1 = (f32[16,1024]{1,0:T(8,128)S(1)}, f32[16,1024]{1,0:T(8,128)S(1)}, u32[]{:S(2)}, u32[]{:S(2)}) collective-permute-start(f32[16,1024]{1,0:T(8,128)S(1)} %get-tuple-element.25), channel_id=1, source_target_pairs={{0,24},{1,25},{2,26},{3,27},{4,28},{5,29},{6,30},{7,31},{8,16},{9,... | collective-permute-start | bytes 196616 | tf_op jit(solution)/shard_map/ppermute | solution.py:454
  80.5 4.2 %weight_grads.1 = (bf16[1024,896]{1,0:T(8,128)(2,1)}, bf16[1024,896]{1,0:T(8,128)(2,1)}, bf16[896,1024]{1,0:T(8,128)(2,1)}) custom-call(bf16[512,1024]{1,0:T(8,128)(2,1)S(1)} %bitcast.9, bf16[512,1024]{1,0:T(8,128)(2,1)S(1)} %bitcast.10, bf16[512,896]{1,0:T(8,128)(2,1)S(1)} %bitcast.11, bf16[512,896]{1,0:T(8,128)(2,1)S(1)} %bitcast.12, ...), custom_call_target="tpu_custom_call" | custom-call | flops 2818572288 | bytes 10354688 | tf_op jit(solution)/shard_map/weight_grads/pallas_call | solution.py:460
  84.7 0.0 collective-permute-done
  84.7 0.0 collective-permute-done.1
  84.7 0.6 add_convert_fusion
  (1 shorter events, 0.0 us)
Async XLA Ops:
  78.1 6.6 %collective-permute-start = (f32[16,1024]{1,0:T(8,128)S(1)}, f32[16,1024]{1,0:T(8,128)S(1)}, u32[]{:S(2)}, u32[]{:S(2)}) collective-permute-start(f32[16,1024]{1,0:T(8,128)S(1)} %get-tuple-element.24), channel_id=1, source_target_pairs={{0,16},{1,17},{2,18},{3,19},{4,20},{5,21},{6,22},{7,23},{8,24},{9,... | collective-permute-start | bytes 196616 | tf_op jit(solution)/shard_map/ppermute | solution.py:454
  78.9 5.8 %collective-permute-start.1 = (f32[16,1024]{1,0:T(8,128)S(1)}, f32[16,1024]{1,0:T(8,128)S(1)}, u32[]{:S(2)}, u32[]{:S(2)}) collective-permute-start(f32[16,1024]{1,0:T(8,128)S(1)} %get-tuple-element.25), channel_id=1, source_target_pairs={{0,24},{1,25},{2,26},{3,27},{4,28},{5,29},{6,30},{7,31},{8,16},{9,... | collective-permute-start | bytes 196616 | tf_op jit(solution)/shard_map/ppermute | solution.py:454

commit v4 on v3

--- a/solution.py
+++ b/solution.py
@@ -43,7 +43,7 @@
 
 def comm_kernel(
     x_hbm, dy_hbm, wg_hbm, wu_hbm, wd_hbm,
-    own_ref, other_ref, xo_hbm, do_hbm, h_hbm, gg_hbm, ug_hbm,
+    own_ref, other_ref, xo_hbm, do_hbm, h_hbm, gu_hbm,
     xd, wg, wu, wd, part, s_far, s_near, s_sum, s_z, r_relay, r_near, r_sum, r_z, grads,
     ig_part, ig_sib, ig_ysend, ig_yrecv, ig_msend, ig_mrecv,
     load_sem, send, recv, p1_send, p1_recv, sib_send, sib_recv, y_send, y_recv,
@@ -236,10 +236,9 @@
     def outs(c):
         return [
             pltpu.make_async_copy(grads.at[c, :, :, pl.ds(0, ff)], h_hbm.at[c], out_sem.at[c, 0]),
-            pltpu.make_async_copy(grads.at[c, :, :, pl.ds(ff, ff)], gg_hbm.at[c], out_sem.at[c, 1]),
-            pltpu.make_async_copy(grads.at[c, :, :, pl.ds(2 * ff, ff)], ug_hbm.at[c], out_sem.at[c, 2]),
-            pltpu.make_async_copy(xd.at[c, :, :, 0], xo_hbm.at[c], out_sem.at[c, 3]),
-            pltpu.make_async_copy(xd.at[c, :, :, 1], do_hbm.at[c], out_sem.at[c, 4]),
+            pltpu.make_async_copy(grads.at[c, :, :, pl.ds(ff, 2 * ff)], gu_hbm.at[c], out_sem.at[c, 1]),
+            pltpu.make_async_copy(xd.at[c, :, :, 0], xo_hbm.at[c], out_sem.at[c, 2]),
+            pltpu.make_async_copy(xd.at[c, :, :, 1], do_hbm.at[c], out_sem.at[c, 3]),
         ]
 
     def ig_to_sibling(c):
@@ -361,23 +360,24 @@
         drain(c)
 
 
-def weight_grad_kernel(
-    xv, dv, hv, gv, uv, gate_hbm, up_hbm, down_hbm, gate_up, down, out_sem,
-):
+def weight_grad_kernel(xv, dv, hv, guv, gate_hbm, up_hbm, down_hbm, gate, up, down, out_sem):
+    ff = hv.shape[1]
     stores = []
 
-    def product(which, lhs, rhs, buffer, target):
-        rows = lhs.shape[1]
-        for i in range(0, rows, 256):
-            part = pl.ds(i, min(256, rows - i))
-            buffer[part] = lax.dot_general(lhs[:, part], rhs[...], TN, preferred_element_type=F32).astype(BF16)
+    def product(lhs, rhs, i, targets):
+        part = pl.ds(i, min(256, lhs.shape[1] - i))
+        total = lax.dot_general(lhs[:, part], rhs[...], TN, preferred_element_type=F32)
+        width = total.shape[1] // len(targets)
+        for n, (which, buffer, target) in enumerate(targets):
+            buffer[part] = total[:, n * width : (n + 1) * width].astype(BF16)
             store = pltpu.make_async_copy(buffer.at[part], target.at[part], out_sem.at[which, i // 256])
             store.start()
             stores.append(store)
 
-    product(0, xv, gv, gate_up.at[0], gate_hbm)
-    product(1, xv, uv, gate_up.at[1], up_hbm)
-    product(2, hv, dv, down, down_hbm)
+    for i in range(0, xv.shape[1], 256):
+        product(xv, guv, i, ((0, gate, gate_hbm), (1, up, up_hbm)))
+    for i in range(0, ff, 256):
+        product(hv, dv, i, ((2, down, down_hbm),))
     for store in stores:
         store.wait()
 
@@ -388,7 +388,7 @@
     anywhere = pl.BlockSpec(memory_space=pltpu.HBM)
     slot = (CHUNKS, 16, 3 * ff)
     dma = pltpu.SemaphoreType.DMA
-    own, other, x_all, d_all, hidden, gate_grad, up_grad = pl.pallas_call(
+    own, other, x_all, d_all, hidden, gate_up_grad = pl.pallas_call(
         comm_kernel,
         out_shape=[
             jax.ShapeDtypeStruct((16, feats), F32),
@@ -396,11 +396,10 @@
             jax.ShapeDtypeStruct((CHUNKS, 2, 2, 16, feats), BF16),
             jax.ShapeDtypeStruct((CHUNKS, 2, 2, 16, feats), BF16),
             jax.ShapeDtypeStruct(blocks + (ff,), BF16),
-            jax.ShapeDtypeStruct(blocks + (ff,), BF16),
-            jax.ShapeDtypeStruct(blocks + (ff,), BF16),
+            jax.ShapeDtypeStruct(blocks + (2 * ff,), BF16),
         ],
         in_specs=[anywhere] * 5,
-        out_specs=[pl.BlockSpec(memory_space=pltpu.VMEM)] * 2 + [anywhere] * 5,
+        out_specs=[pl.BlockSpec(memory_space=pltpu.VMEM)] * 2 + [anywhere] * 4,
         scratch_shapes=[
             pltpu.VMEM((CHUNKS, 2, 2, 2, 16, feats), BF16),
             pltpu.VMEM((feats, ff), BF16),
@@ -437,7 +436,7 @@
             dma((6,)),
             dma(()),
             dma(()),
-            dma((CHUNKS, 5)),
+            dma((CHUNKS, 4)),
             pltpu.SemaphoreType.REGULAR((6,)),
         ],
         compiler_params=pltpu.CompilerParams(
@@ -464,10 +463,11 @@
             jax.ShapeDtypeStruct((feats, ff), BF16),
             jax.ShapeDtypeStruct((ff, feats), BF16),
         ],
-        in_specs=[pl.BlockSpec(memory_space=pltpu.VMEM)] * 5,
+        in_specs=[pl.BlockSpec(memory_space=pltpu.VMEM)] * 4,
         out_specs=[anywhere] * 3,
         scratch_shapes=[
-            pltpu.VMEM((2, feats, ff), BF16),
+            pltpu.VMEM((feats, ff), BF16),
+            pltpu.VMEM((feats, ff), BF16),
             pltpu.VMEM((ff, feats), BF16),
             dma((3, 4)),
         ],
@@ -478,7 +478,7 @@
             transcendentals=0,
         ),
         name="weight_grads",
-    )(flat(x_all), flat(d_all), flat(hidden), flat(gate_grad), flat(up_grad))
+    )(flat(x_all), flat(d_all), flat(hidden), flat(gate_up_grad))
     input_grad = (own + from_far[0] + from_far[1]).astype(BF16)
     return input_grad, gate_weight_grad, up_weight_grad, down_weight_grad
 

time: 85.6 us -> 85.5 us (level)
  no operation moved by 1% of the time
where the time goes in v4:
time: 85.5 us; the launch traced here: 85 us
  Pallas kernels  81.2 us (95%)
  starting transfers between devices  2.44 us (3%)
    pallas_call x1, Pallas kernels, body(): pl.pallas_call(comm_kernel, out_shape=[jax.ShapeDtypeStruct((16, feats),...  77.3 us
    pallas_call x1, Pallas kernels, body(): pl.pallas_call(weight_grad_kernel, out_shape=[jax.ShapeDtypeStruct((feats...  3.89 us
    ppermute x2, starting transfers between devices, body(): lax.ppermute(other[i], 'col', [far(i, col) for col in range(32)])  2.44 us
  transfers between devices with their start and end apart: 2, of which 0 were waited for; matrix products, arithmetic and copies ran while one was open for 0% of the time, Pallas kernels for 5%

profile of v4, /device:TPU:1, one launch (start us, length us, event | category | flops | bytes accessed | tf_op | source)
XLA Modules:
  0.0 85.0 jit_solution(1155291802617864180)
XLA Ops:
  0.6 77.3 %comm.1 = (f32[16,1024]{1,0:T(8,128)S(1)}, f32[2,16,1024]{2,1,0:T(8,128)S(1)}, bf16[8,2,2,16,1024]{4,3,2,1,0:T(8,128)(2,1)S(1)}, bf16[8,2,2,16,1024]{4,3,2,1,0:T...) custom-call(bf16[16,1024]{1,0:T(8,128)(2,1)} %x_hbm.1, ...), custom_call_target="tpu_custom_call" | custom-call | tf_op jit(solution)/shard_map/comm/pallas_call | solution.py:391
  78.0 0.8 collective-permute-start
  78.8 1.6 %collective-permute-start.1 = (f32[16,1024]{1,0:T(8,128)S(1)}, f32[16,1024]{1,0:T(8,128)S(1)}, u32[]{:S(2)}, u32[]{:S(2)}) collective-permute-start(f32[16,1024]{1,0:T(8,128)S(1)} %get-tuple-element.23), channel_id=1, source_target_pairs={{0,24},{1,25},{2,26},{3,27},{4,28},{5,29},{6,30},{7,31},{8,16},{9,... | collective-permute-start | bytes 196616 | tf_op jit(solution)/shard_map/ppermute | solution.py:453
  80.4 3.9 %weight_grads.1 = (bf16[1024,896]{1,0:T(8,128)(2,1)}, bf16[1024,896]{1,0:T(8,128)(2,1)}, bf16[896,1024]{1,0:T(8,128)(2,1)}) custom-call(bf16[512,1024]{1,0:T(8,128)(2,1)S(1)} %bitcast.9, bf16[512,1024]{1,0:T(8,128)(2,1)S(1)} %bitcast.10, bf16[512,896]{1,0:T(8,128)(2,1)S(1)} %bitcast.11, bf16[512,1792]{1,0:T(8,128)(2,1)S(1)} %bitcast.8), custom_call_target="tpu_custom_call" | custom-call | flops 2818572288 | bytes 10354688 | tf_op jit(solution)/shard_map/weight_grads/pallas_call | solution.py:459
  84.3 0.0 collective-permute-done
  84.3 0.0 collective-permute-done.1
  84.3 0.6 add_convert_fusion
  (1 shorter events, 0.0 us)
Async XLA Ops:
  78.0 6.3 %collective-permute-start = (f32[16,1024]{1,0:T(8,128)S(1)}, f32[16,1024]{1,0:T(8,128)S(1)}, u32[]{:S(2)}, u32[]{:S(2)}) collective-permute-start(f32[16,1024]{1,0:T(8,128)S(1)} %get-tuple-element.22), channel_id=1, source_target_pairs={{0,16},{1,17},{2,18},{3,19},{4,20},{5,21},{6,22},{7,23},{8,24},{9,... | collective-permute-start | bytes 196616 | tf_op jit(solution)/shard_map/ppermute | solution.py:453
  78.8 5.5 %collective-permute-start.1 = (f32[16,1024]{1,0:T(8,128)S(1)}, f32[16,1024]{1,0:T(8,128)S(1)}, u32[]{:S(2)}, u32[]{:S(2)}) collective-permute-start(f32[16,1024]{1,0:T(8,128)S(1)} %get-tuple-element.23), channel_id=1, source_target_pairs={{0,24},{1,25},{2,26},{3,27},{4,28},{5,29},{6,30},{7,31},{8,16},{9,... | collective-permute-start | bytes 196616 | tf_op jit(solution)/shard_map/ppermute | solution.py:453
